TPU v7x, 32 devices: a whole 2x2x4 slice. The times are simulated.
32 devices in a mesh: scenes: 2 (over y), rows: 4 (over x, core), cols: 4 (over z).
Axes of the slice: x: 2, y: 2, z: 4, core: 2. Of those that a mesh axis runs over, the one named last changes fastest.
Arguments:
- features: bfloat16 [256, 64, 256], P(('scenes', 'rows'), 'cols'), parts along dimension 0, may hold values from -100 to 100
- dw_kernel: bfloat16 [7, 7, 256], replicated, may hold values from -0.875 to 0.875
- norm_gain: float32 [256], replicated, may hold values from 0.1 to 1.9
- query_state: bfloat16 [600, 256], P('scenes'), parts along dimension 0, may hold values from -6 to 6
- query_pos: bfloat16 [600, 256], P('scenes'), parts along dimension 0, may hold values from -175 to 175
- w_query: bfloat16 [256, 256], replicated, may hold values from -0.375 to 0.375
- w_key: bfloat16 [256, 256], replicated, may hold values from -0.375 to 0.375
- w_value: bfloat16 [256, 256], replicated, may hold values from -0.375 to 0.375
- w_out: bfloat16 [256, 256], replicated, may hold values from -0.375 to 0.375
Outputs:
- memory: bfloat16 [256, 64, 256], P(('scenes', 'rows'), 'cols'), parts along dimension 0
- decoded: float32 [600, 256], P('scenes'), parts along dimension 0
There are 2 independent parts, one for each index of `scenes`. A program takes and returns all parts, laid end to end along the dimension named above; an argument that names none is the same for every part. Nothing has to cross between parts.
All inputs are finite; a program needn't handle non-finite values.
Results may differ from a plain program's by a relative error of at most 0.0024.
The roundings to bfloat16 on the way count: a program that leaves them out, or rounds other values in their place, can miss the bound.
Values may be sent and summed in bfloat16 or wider, within the bound.
A program may use at most 64 MiB of HBM per device.

v0:
```python
import jax
import jax.numpy as jnp
from jax import lax
from jax.sharding import PartitionSpec as P

HEADS = 8


def with_halo(value, sides, width):
    for axis, dim in sides:
        size, length = (lax.axis_size(axis), value.shape[dim])
        up = [(i, (i + 1) % size) for i in range(size - 1)]
        down = [(j, i) for i, j in up]
        last = lax.slice_in_dim(value, length - width, length, axis=dim)
        initial = lax.slice_in_dim(value, 0, width, axis=dim)
        before = lax.ppermute(last, axis, up)
        after = lax.ppermute(initial, axis, down)
        value = jnp.concatenate([before, value, after], axis=dim)
    return value


def layer_norm(vector):
    centred = vector - jnp.mean(vector, axis=-1, keepdims=True)
    variance = jnp.mean(centred * centred, axis=-1, keepdims=True)
    return centred * lax.rsqrt(variance + 1e-06)


def body(features, dw_kernel, norm_gain, query_state, query_pos, w_query, w_key, w_value, w_out):
    tile_rows, tile_cols, width = features.shape
    head_dim = width // HEADS
    row_padded = with_halo(features, (("rows", 0),), 3)
    padded = with_halo(row_padded, (("cols", 1),), 3)
    kernel = dw_kernel.astype(jnp.float32)
    conv = jnp.zeros((tile_rows, tile_cols, width), jnp.float32)
    for offset_row in range(7):
        for offset_col in range(7):
            window = padded[
                offset_row : offset_row + tile_rows, offset_col : offset_col + tile_cols, :
            ]
            conv = conv + window.astype(jnp.float32) * kernel[offset_row, offset_col]
    memory = (features.astype(jnp.float32) + layer_norm(conv) * norm_gain).astype(jnp.bfloat16)
    flat = memory.reshape(tile_rows * tile_cols, width)
    keys = jnp.dot(flat, w_key, preferred_element_type=jnp.float32).astype(jnp.bfloat16)
    values = jnp.dot(flat, w_value, preferred_element_type=jnp.float32).astype(jnp.bfloat16)
    mixed = (query_state.astype(jnp.float32) + query_pos.astype(jnp.float32)).astype(jnp.bfloat16)
    queries = (
        jnp.dot(mixed, w_query, preferred_element_type=jnp.float32) * head_dim ** (-0.5)
    ).astype(jnp.bfloat16)
    max_list = []
    total_list = []
    sum_list = []
    for head_index in range(HEADS):
        low = head_index * head_dim
        scores = lax.dot_general(
            queries[:, low : low + head_dim],
            keys[:, low : low + head_dim],
            (((1,), (1,)), ((), ())),
            preferred_element_type=jnp.float32,
        )
        local_max = jnp.max(scores, axis=-1)
        expo = jnp.exp(scores - local_max[:, None])
        total_list.append(jnp.sum(expo, axis=-1))
        max_list.append(local_max)
        sum_list.append(
            jnp.dot(
                expo.astype(jnp.bfloat16),
                values[:, low : low + head_dim],
                preferred_element_type=jnp.float32,
            )
        )
    maxima = jnp.stack(max_list, axis=1)
    totals = jnp.stack(total_list, axis=1)
    sums = jnp.concatenate(sum_list, axis=1)

    def widen(factor):
        return jnp.repeat(factor, head_dim, axis=1)

    global_max = lax.pmax(maxima, ("rows", "cols"))
    rescale = jnp.exp(maxima - global_max)
    totals, sums = lax.psum((totals * rescale, sums * widen(rescale)), ("rows", "cols"))
    attended = (sums / widen(totals)).astype(jnp.bfloat16)
    projected = jnp.dot(attended, w_out, preferred_element_type=jnp.float32)
    decoded = layer_norm(query_state.astype(jnp.float32) + projected)
    return (memory, decoded)


def solution(mesh):
    in_specs = (
        P(("scenes", "rows"), "cols", None),
        P(),
        P(),
        P("scenes", None),
        P("scenes", None),
        P(),
        P(),
        P(),
        P(),
    )
    out_specs = (P(("scenes", "rows"), "cols", None), P("scenes", None))
    return jax.shard_map(body, mesh=mesh, in_specs=in_specs, out_specs=out_specs, check_vma=False)
```

profile of v0, /device:TPU:0, one launch (start us, length us, event | category | flops | bytes accessed | tf_op | source)
XLA Modules:
  0.0 220.0 jit_solution(14849400195409667426)
XLA Ops:
  7.2 0.8 fusion.138
  8.0 2.3 %collective-permute-start = (bf16[3,16,256]{2,1,0:T(8,128)(2,1)S(1)}, bf16[3,16,256]{2,1,0:T(8,128)(2,1)S(1)}, u32[]{:S(2)}, u32[]{:S(2)}) collective-permute-start(bf16[3,16,256]{2,1,0:T(8,128)(2,1)S(1)} %get-tuple-element.12), channel_id=1, source_target_pairs={{0,4},{4,8},{8,12},{1,5},{5,9},{9,13},{2,6},{6,10},{10,14},{3,7},{... | collective-permute-start | bytes 73736 | tf_op jit(solution)/shard_map/ppermute | solution.py:16
  10.4 1.3 collective-permute-start.1
  11.7 1.0 fusion.139
  12.7 1.2 fusion
  14.1 1.5 collective-permute-done.1
  15.7 3.5 %collective-permute-start.2 = (bf16[38,3,256]{2,1,0:T(4,128)(2,1)S(1)}, bf16[38,3,256]{2,1,0:T(4,128)(2,1)S(1)}, u32[]{:S(2)}, u32[]{:S(2)}) collective-permute-start(bf16[38,3,256]{2,1,0:T(4,128)(2,1)S(1)} %get-tuple-element.6), channel_id=1, source_target_pairs={{0,1},{1,2},{2,3},{4,5},{5,6},{6,7},{8,9},{9,10},{10,11},{12,13},{... | collective-permute-start | bytes 175112 | tf_op jit(solution)/shard_map/ppermute | solution.py:16
  19.1 1.3 collective-permute-start.3
  20.5 0.7 collective-permute-done.2
  21.1 4.3 %collective-permute-done.3 = bf16[38,3,256]{2,1,0:T(4,128)(2,1)S(1)} collective-permute-done((bf16[38,3,256]{2,1,0:T(4,128)(2,1)S(1)}, bf16[38,3,256]{2,1,0:T(4,128)(2,1)S(1)}, u32[]{:S(2)}, u32[]{:S(2)}) %collective-permute-start.3) | collective-permute-done | bytes 58400 | tf_op jit(solution)/shard_map/ppermute | solution.py:17
  25.4 6.2 %fusion.135 = (f32[32,16]{1,0:T(8,128)S(1)}, f32[32,16,256]{2,1,0:T(8,128)S(1)}) fusion(f32[256]{0:T(256)S(1)} %bitcast.113, bf16[38,3,256]{2,1,0:T(4,128)(2,1)S(1)} %collective-permute-done.3, bf16[38,16,256]{2,1,0:T(8,128)(2,1)S(1)} %get-tuple-element.65, f32[256]{0:T(256)S(1)} %bitcast.112, f32[256]{0:T(256)S(1)} %bitcast.111, f32[256]{0:T(256)S(1)} %bitcast.110, ...), kind=kLoop, calls=%fused_computation.248 | loop fusion | flops 35782144 | bytes 2839552 | tf_op jit(solution)/shard_map/reduce_sum | solution.py:23
  31.9 0.7 copy-done.23
  33.1 1.0 fusion.142
  34.1 1.1 fusion.143
  35.2 1.1 fusion.144
  37.1 0.4 fusion.147
  37.4 0.4 fusion.148
  38.3 0.6 broadcast_in_dim.38
  38.8 0.6 broadcast_in_dim.39
  39.4 0.6 broadcast_in_dim.40
  40.0 0.6 broadcast_in_dim.41
  40.6 0.6 broadcast_in_dim.42
  41.2 0.7 stack.38
  41.9 59.7 %pmax.7 = f32[300,8]{0,1:T(8,128)S(1)} all-reduce(f32[300,8]{0,1:T(8,128)S(1)} %stack.38), channel_id=1, replica_groups=mesh['scenes'=2,'rows'=4,'cols'=4] {'rows','cols'}, use_global_device_ids=true, to_apply=%region_10.0 | all-reduce | flops 2400 | bytes 19200 | tf_op jit(solution)/shard_map/pmax | solution.py:78
  101.6 1.4 fusion.1
  103.0 0.6 stack.39
  103.6 0.9 fusion.3
  104.5 0.6 stack.40
  105.3 0.6 stack.41
  106.2 0.6 stack.42
  107.0 0.6 stack.43
  107.9 0.5 stack.44
  108.7 0.6 stack.45
  109.5 0.6 stack.46
  110.4 0.4 copy-done.12
  110.8 0.9 convolution_dynamic-update-slice_fusion.7
  111.7 0.9 convolution_dynamic-update-slice_fusion.6
  112.6 0.9 convolution_dynamic-update-slice_fusion.5
  113.5 0.9 convolution_dynamic-update-slice_fusion.4
  114.4 0.9 convolution_dynamic-update-slice_fusion.3
  115.3 0.9 convolution_dynamic-update-slice_fusion.2
  116.2 0.9 convolution_dynamic-update-slice_fusion.1
  117.2 0.9 convolution_dynamic-update-slice_fusion
  118.2 1.8 bitcast_multiply_fusion
  120.0 58.2 %psum.15 = f32[300,8]{0,1:T(8,128)S(1)} all-reduce(f32[300,8]{0,1:T(8,128)S(1)} %get-tuple-element.2), channel_id=1, replica_groups=mesh['scenes'=2,'rows'=4,'cols'=4] {'rows','cols'}, use_global_device_ids=true, to_apply=%region_20.0 | all-reduce | flops 2400 | bytes 19200 | tf_op jit(solution)/shard_map/psum | solution.py:80
  178.2 32.4 %all-reduce.2.cloned.1.call-done = f32[300,256]{0,1:T(8,128)} async-done(((f32[300,256]{0,1:T(8,128)}), f32[300,256]{0,1:T(8,128)}) %all-reduce.2.cloned.1.call-update) | async-done | bytes 307216 | tf_op jit(solution)/shard_map/psum | solution.py:80
  210.6 1.0 fusion.43
  212.2 0.9 subtract_multiply_fusion
  (79 shorter events, 4.6 us)
Async XLA Ops:
  7.2 25.6 %copy-start = (bf16[256,256]{1,0:T(8,128)(2,1)S(1)}, bf16[256,256]{1,0:T(8,128)(2,1)}, u32[]{:S(2)}) copy-start(bf16[256,256]{1,0:T(8,128)(2,1)} %param.15) | copy-start | bytes 393220
  7.2 5.5 %copy-start.9 = (bf16[256,256]{1,0:T(8,128)(2,1)S(1)}, bf16[256,256]{1,0:T(8,128)(2,1)}, u32[]{:S(2)}) copy-start(bf16[256,256]{1,0:T(8,128)(2,1)} %param.14) | copy-start | bytes 393220
  7.2 203.4 %all-reduce.2.cloned.1.call-start = ((), (), s32[]{:S(2)}) async-start(), calls=%async_computation | async-start | bytes 786432 | tf_op jit(solution)/shard_map/psum | solution.py:80
  8.0 6.0 %collective-permute-start = (bf16[3,16,256]{2,1,0:T(8,128)(2,1)S(1)}, bf16[3,16,256]{2,1,0:T(8,128)(2,1)S(1)}, u32[]{:S(2)}, u32[]{:S(2)}) collective-permute-start(bf16[3,16,256]{2,1,0:T(8,128)(2,1)S(1)} %get-tuple-element.12), channel_id=1, source_target_pairs={{0,4},{4,8},{8,12},{1,5},{5,9},{9,13},{2,6},{6,10},{10,14},{3,7},{... | collective-permute-start | bytes 73736 | tf_op jit(solution)/shard_map/ppermute | solution.py:16
  10.4 5.2 %collective-permute-start.1 = (bf16[3,16,256]{2,1,0:T(8,128)(2,1)S(1)}, bf16[3,16,256]{2,1,0:T(8,128)(2,1)S(1)}, u32[]{:S(2)}, u32[]{:S(2)}) collective-permute-start(bf16[3,16,256]{2,1,0:T(8,128)(2,1)S(1)} %get-tuple-element.11), channel_id=1, source_target_pairs={{4,0},{8,4},{12,8},{5,1},{9,5},{13,9},{6,2},{10,6},{14,10},{7,3},{... | collective-permute-start | bytes 73736 | tf_op jit(solution)/shard_map/ppermute | solution.py:17
  12.7 1.3 copy-start.10
  12.7 1.3 copy-start.4
  15.7 5.5 %collective-permute-start.2 = (bf16[38,3,256]{2,1,0:T(4,128)(2,1)S(1)}, bf16[38,3,256]{2,1,0:T(4,128)(2,1)S(1)}, u32[]{:S(2)}, u32[]{:S(2)}) collective-permute-start(bf16[38,3,256]{2,1,0:T(4,128)(2,1)S(1)} %get-tuple-element.6), channel_id=1, source_target_pairs={{0,1},{1,2},{2,3},{4,5},{5,6},{6,7},{8,9},{9,10},{10,11},{12,13},{... | collective-permute-start | bytes 175112 | tf_op jit(solution)/shard_map/ppermute | solution.py:16
  19.1 6.3 %collective-permute-start.3 = (bf16[38,3,256]{2,1,0:T(4,128)(2,1)S(1)}, bf16[38,3,256]{2,1,0:T(4,128)(2,1)S(1)}, u32[]{:S(2)}, u32[]{:S(2)}) collective-permute-start(bf16[38,3,256]{2,1,0:T(4,128)(2,1)S(1)} %get-tuple-element.7), channel_id=1, source_target_pairs={{1,0},{2,1},{3,2},{5,4},{6,5},{7,6},{9,8},{10,9},{11,10},{13,12},{... | collective-permute-start | bytes 175112 | tf_op jit(solution)/shard_map/ppermute | solution.py:17
  31.9 0.7 copy-start.23
  32.8 77.3 %copy-start.5 = (bf16[32,16,256]{2,1,0:T(8,128)(2,1)}, bf16[32,16,256]{2,1,0:T(8,128)(2,1)S(1)}, u32[]{:S(2)}) copy-start(bf16[32,16,256]{2,1,0:T(8,128)(2,1)S(1)} %fusion.42) | copy-start | bytes 786436
  34.1 4.1 %copy-start.11 = (f32[300]{0:T(512)}, f32[300]{0:T(512)S(1)}, u32[]{:S(2)}) copy-start(f32[300]{0:T(512)S(1)} %get-tuple-element.66) | copy-start | bytes 3604
  35.2 3.0 %copy-start.13 = (f32[300]{0:T(512)}, f32[300]{0:T(512)S(1)}, u32[]{:S(2)}) copy-start(f32[300]{0:T(512)S(1)} %get-tuple-element.68) | copy-start | bytes 3604
  101.5 2.0 copy-start.3
  101.5 3.5 %copy-start.1 = (f32[300,512]{1,0:T(8,128)S(1)}, f32[300,512]{1,0:T(8,128)}, u32[]{:S(2)}) copy-start(f32[300,512]{1,0:T(8,128)} %get-tuple-element.71) | copy-start | bytes 1843204
  108.4 1.7 copy-start.7
  109.2 1.1 copy-start.2
  110.1 0.7 copy-start.12
  110.8 0.9 copy-start.14
  117.1 1.0 copy-start.15
  117.1 1.0 copy-start.16
  117.2 1.0 copy-start.17
  117.2 1.0 copy-start.18
  117.2 1.0 copy-start.19
  117.2 1.0 copy-start.20
  117.2 1.0 copy-start.21
  117.2 1.0 copy-start.22
  178.2 33.4 %copy-start.6 = (bf16[300,256]{1,0:T(8,128)(2,1)S(1)}, bf16[300,256]{1,0:T(8,128)(2,1)}, u32[]{:S(2)}) copy-start(bf16[300,256]{1,0:T(8,128)(2,1)} %param.12) | copy-start | bytes 460804
  178.2 33.5 %copy-start.8 = (bf16[256,256]{1,0:T(8,128)(2,1)S(1)}, bf16[256,256]{1,0:T(8,128)(2,1)}, u32[]{:S(2)}) copy-start(bf16[256,256]{1,0:T(8,128)(2,1)} %param.17) | copy-start | bytes 393220
Sparse Core Ops, SparseCore 0:
  120.1 90.4 all-reduce.1
where the time goes:
time: 220 us
  blocking collectives  118 us (54%)
  waiting for transfers between devices  38.9 us (18%)
  matrix products  14.5 us (7%)
  other arithmetic  14.5 us (7%)
  between operations  14.4 us (7%)
  local copies, waits for them, and re-layouts  11.4 us (5%)
  starting transfers between devices  8.45 us (4%)
    pmax x1, blocking collectives, body(): global_max = lax.pmax(maxima, ('rows', 'cols'))  59.7 us
    psum x1, blocking collectives, body(): lax.psum((totals * rescale, sums * widen(rescale)), ('rows', 'cols'))  58.2 us
    psum x1, waiting for transfers between devices, body(): lax.psum((totals * rescale, sums * widen(rescale)), ('rows', 'cols'))  32.4 us
    dot_general x8, matrix products, body(): jnp.dot(expo.astype(jnp.bfloat16), values[:, low:low + head_dim], preferr...  7.25 us
    reduce_sum x1, other arithmetic, layer_norm(): centred = vector - jnp.mean(vector, axis=-1, keepdims=True)  6.16 us
    ppermute x2, starting transfers between devices, with_halo(): before = lax.ppermute(last, axis, up)  5.83 us
    ppermute x2, waiting for transfers between devices, with_halo(): after = lax.ppermute(initial, axis, down)  5.76 us
    dot_general x8, matrix products, body(): lax.dot_general(queries[:, low:low + head_dim], keys[:, low:low + head_di...  5.14 us
  transfers between devices with their start and end apart: 5, of which 4 were waited for; matrix products, arithmetic and copies ran while one was open for 1% of the time, Pallas kernels for 0%

commit v1 on v0

v1 whole, which is shorter than its diff:
```python
import functools
import jax
import jax.numpy as jnp
from jax import lax
from jax.experimental import pallas as pl
from jax.experimental.pallas import tpu as pltpu
from jax.sharding import PartitionSpec as P

HEADS = 8
SCATTER = "rows"
EXCHANGE = "cols"
MESH = pl.DeviceIdType.MESH
F32 = jnp.float32
BF16 = jnp.bfloat16
STATS = 128

DIRS = ((-1, 0), (1, 0), (0, -1), (0, 1), (-1, -1), (-1, 1), (1, -1), (1, 1))


def iota(shape, dim):
    return lax.broadcasted_iota(jnp.int32, shape, dim)


def layer_norm(vector):
    centred = vector - jnp.mean(vector, axis=-1, keepdims=True)
    variance = jnp.mean(centred * centred, axis=-1, keepdims=True)
    return centred * lax.rsqrt(variance + 1e-06)


def dot(a, b):
    return jnp.dot(a, b, preferred_element_type=F32)


def split(value, terms):
    parts = []
    for _ in range(terms):
        part = value.astype(BF16)
        parts.append(part)
        value = value - part.astype(F32)
    return parts


def pack(out_ref, sums, maxima, totals):
    width = sums.shape[1]
    head_dim = width // HEADS
    out_ref[:, :width] = sums.astype(BF16)
    src, lane = iota((width, STATS), 0), iota((width, STATS), 1)
    stats = None
    for group, part in enumerate(split(maxima, 3) + split(totals, 3)):
        pick = (src == (lane - group * HEADS) * head_dim) & (lane >= group * HEADS)
        pick = pick & (lane < (group + 1) * HEADS)
        term = dot(part, jnp.where(pick, 1.0, 0.0).astype(BF16))
        stats = term if stats is None else stats + term
    out_ref[:, width:] = stats.astype(BF16)


def unpack(in_ref, width):
    head_dim = width // HEADS
    sums = in_ref[:, :width].astype(F32)
    stats = in_ref[:, width:]
    lane, chan = iota((STATS, width), 0), iota((STATS, width), 1)
    results = [sums]
    for first in (0, 3 * HEADS):
        pick = None
        for group in range(3):
            head = lane - (first + group * HEADS)
            hit = (chan >= head * head_dim) & (chan < (head + 1) * head_dim)
            hit = hit & (head >= 0) & (head < HEADS)
            pick = hit if pick is None else pick | hit
        results.append(dot(stats, jnp.where(pick, 1.0, 0.0).astype(BF16)))
    return results


def combine(parts):
    top = parts[0][1]
    for _, maxima, _ in parts[1:]:
        top = jnp.maximum(top, maxima)
    sums, totals = None, None
    for part_sums, maxima, part_totals in parts:
        scale = jnp.exp(maxima - top)
        s, t = part_sums * scale, part_totals * scale
        sums = s if sums is None else sums + s
        totals = t if totals is None else totals + t
    return sums, top, totals


def kernel(
    sizes, feat, dwk, gain, qs, qp, wq, wk, wv, wo, mem, dec,
    pad, dwf, conv, packed, rowrecv, colrecv, cornrecv, keys, values, qf, queries,
    p1send, p1recv, p2send, p2recv, attended,
    hsend, hrecv, s1, r1, s2, r2, s3, r3,
):
    n_rows, n_cols = sizes["rows"], sizes["cols"]
    n_a, n_b = sizes[SCATTER], sizes[EXCHANGE]
    tile_rows, tile_cols, width = feat.shape
    pixels = tile_rows * tile_cols
    n_query = qs.shape[0]
    block = p2send.shape[0]
    head_dim = width // HEADS
    row, col = lax.axis_index("rows"), lax.axis_index("cols")
    me_a, me_b = lax.axis_index(SCATTER), lax.axis_index(EXCHANGE)

    barrier = pltpu.get_barrier_semaphore()
    for k in range(1, n_a):
        pl.semaphore_signal(
            barrier, inc=1, device_id={SCATTER: lax.rem(me_a + k, n_a)}, device_id_type=MESH
        )
    for k in range(1, n_b):
        pl.semaphore_signal(
            barrier, inc=1, device_id={EXCHANGE: lax.rem(me_b + k, n_b)}, device_id_type=MESH
        )
    for dr, dc in DIRS[4:]:
        pl.semaphore_signal(
            barrier, inc=1,
            device_id={
                "rows": lax.rem(row + dr + n_rows, n_rows),
                "cols": lax.rem(col + dc + n_cols, n_cols),
            },
            device_id_type=MESH,
        )

    flat_in = feat[...].reshape(pixels, width)
    pieces = []
    for first in (0, tile_cols - 3):
        for j in range(3):
            want = iota((tile_rows, pixels), 0) * tile_cols + (first + j)
            pieces.append(want == iota((tile_rows, pixels), 1))
    for dr, dc in DIRS[4:]:
        k = iota((16, pixels), 0)
        i, j = k >> 2, k & 3
        r0 = 0 if dr < 0 else tile_rows - 3
        c0 = 0 if dc < 0 else tile_cols - 3
        want = (r0 + i) * tile_cols + c0 + j
        pieces.append((want == iota((16, pixels), 1)) & (i < 3) & (j < 3))
    select = jnp.concatenate([jnp.where(p, 1.0, 0.0).astype(BF16) for p in pieces], axis=0)
    packed[...] = dot(select, flat_in).astype(BF16)

    pl.semaphore_wait(barrier, (n_a - 1) + (n_b - 1) + 4)

    def halo(index):
        dr, dc = DIRS[index]
        if index < 2:
            src = feat.at[pl.ds(0 if dr < 0 else tile_rows - 3, 3)]
            dst = rowrecv.at[index]
        elif index < 4:
            src = packed.at[pl.ds((index - 2) * 3 * tile_rows, 3 * tile_rows)]
            dst = colrecv.at[index - 2]
        else:
            src = packed.at[pl.ds(6 * tile_rows + (index - 4) * 16, 16)]
            dst = cornrecv.at[index - 4]
        there = (
            (row + dr >= 0) & (row + dr < n_rows) & (col + dc >= 0) & (col + dc < n_cols)
        )
        comes = (
            (row - dr >= 0) & (row - dr < n_rows) & (col - dc >= 0) & (col - dc < n_cols)
        )
        copy = pltpu.make_async_remote_copy(
            src_ref=src, dst_ref=dst, send_sem=hsend.at[index], recv_sem=hrecv.at[index],
            device_id={"rows": row + dr, "cols": col + dc}, device_id_type=MESH,
        )
        return copy, there, comes, dst

    halos = [halo(i) for i in range(8)]
    for index in (2, 3, 4, 5, 6, 7, 0, 1):
        copy, there, comes, dst = halos[index]

        @pl.when(there)
        def _():
            copy.start()

        @pl.when(jnp.logical_not(comes))
        def _():
            dst[...] = jnp.zeros(dst.shape, BF16)

    pad[pl.ds(3, tile_rows), 8 : 8 + tile_cols, :] = feat[...].astype(F32)
    dwf[...] = dwk[...].astype(F32)
    mixed = (qs[...].astype(F32) + qp[...].astype(F32)).astype(BF16)
    qf[...] = jnp.zeros(qf.shape, F32)
    qf[0:n_query, :] = dot(mixed, wq[...]) * head_dim ** (-0.5)
    queries[...] = qf[...].astype(BF16)

    for index in range(8):
        copy, there, comes, dst = halos[index]

        @pl.when(comes)
        def _():
            copy.wait_recv()

    for index in range(2):
        at = 0 if DIRS[index][0] > 0 else tile_rows + 3
        pad[at : at + 3, 8 : 8 + tile_cols, :] = rowrecv[index].astype(F32)
    for index in range(2, 4):
        k, q = iota((tile_rows * 8, 3 * tile_rows), 1), iota((tile_rows * 8, 3 * tile_rows), 0)
        j = jnp.where(k >= tile_rows, 1, 0) + jnp.where(k >= 2 * tile_rows, 1, 0)
        left = DIRS[index][1] > 0
        hit = q == (k - j * tile_rows) * 8 + j + (5 if left else 0)
        slab = dot(jnp.where(hit, 1.0, 0.0).astype(BF16), colrecv[index - 2])
        at = 0 if left else 8 + tile_cols
        pad[3 : 3 + tile_rows, at : at + 8, :] = slab.reshape(tile_rows, 8, width)
    for index in range(4, 8):
        k, q = iota((24, 16), 1), iota((24, 16), 0)
        left = DIRS[index][1] > 0
        hit = (q == (k >> 2) * 8 + (k & 3) + (5 if left else 0)) & (k < 12) & ((k & 3) < 3)
        slab = dot(jnp.where(hit, 1.0, 0.0).astype(BF16), cornrecv[index - 4])
        up = 0 if DIRS[index][0] > 0 else tile_rows + 3
        at = 0 if left else 8 + tile_cols
        pad[up : up + 3, at : at + 8, :] = slab.reshape(3, 8, width)

    chunk = 8
    scale = gain[...]

    def conv_chunk(step, carry):
        r0 = step * chunk
        for g in range(tile_cols // 8):
            acc = [jnp.zeros((8, width), F32) for _ in range(chunk)]
            for dc in range(7):
                taps = [
                    jnp.broadcast_to(dwf[dr, dc : dc + 1, :], (8, width)) for dr in range(7)
                ]
                for i in range(chunk + 6):
                    x = pad[r0 + i, 5 + dc + 8 * g : 13 + dc + 8 * g, :]
                    for dr in range(7):
                        o = i - dr
                        if 0 <= o < chunk:
                            acc[o] = acc[o] + x * taps[dr]
            for o in range(chunk):
                conv[o, 8 * g : 8 * g + 8, :] = acc[o]
        normed = layer_norm(conv[...].reshape(chunk * tile_cols, width))
        image = feat[pl.ds(r0, chunk)].astype(F32).reshape(chunk * tile_cols, width)
        result = (image + normed * scale).astype(BF16)
        mem[pl.ds(r0, chunk)] = result.reshape(chunk, tile_cols, width)
        return carry

    lax.fori_loop(0, tile_rows // chunk, conv_chunk, 0)

    flat = mem[...].reshape(pixels, width)
    keys[...] = dot(flat, wk[...]).astype(BF16)
    values[...] = dot(flat, wv[...]).astype(BF16)

    def attend(index):
        q = queries[pl.ds(pl.multiple_of(index * block, 16), block), :]
        head_of = iota((block, width), 1) // head_dim
        spread = jnp.concatenate(
            [jnp.where(head_of == h, q, jnp.zeros_like(q)) for h in range(HEADS)], axis=0
        )
        scores = lax.dot_general(
            spread, keys[...], (((1,), (1,)), ((), ())), preferred_element_type=F32
        )
        top = jnp.max(scores, axis=-1, keepdims=True)
        expo = jnp.exp(scores - top)
        total = jnp.sum(expo, axis=-1, keepdims=True)
        out = dot(expo.astype(BF16), values[...])
        sums = jnp.zeros((block, width), F32)
        maxima = jnp.zeros((block, width), F32)
        totals = jnp.zeros((block, width), F32)
        for h in range(HEADS):
            rows = slice(h * block, (h + 1) * block)
            here = head_of == h
            sums = jnp.where(here, out[rows], sums)
            maxima = jnp.where(here, top[rows], maxima)
            totals = jnp.where(here, total[rows], totals)
        return sums, maxima, totals

    def p1(k):
        return pltpu.make_async_remote_copy(
            src_ref=p1send.at[k - 1], dst_ref=p1recv.at[k - 1],
            send_sem=s1.at[k - 1], recv_sem=r1.at[k - 1],
            device_id={SCATTER: lax.rem(me_a + k, n_a)}, device_id_type=MESH,
        )

    def scatter_step(step, carry):
        k = step + 1
        pack(p1send.at[step], *attend(lax.rem(me_a + k, n_a)))
        p1(k).start()
        return carry

    lax.fori_loop(0, n_a - 1, scatter_step, 0)
    parts = [attend(me_a)]
    for k in range(1, n_a):
        p1(k).wait_recv()
        parts.append(unpack(p1recv.at[k - 1], width))
    mine = combine(parts)
    pack(p2send, *mine)

    def p2(k):
        return pltpu.make_async_remote_copy(
            src_ref=p2send, dst_ref=p2recv.at[k - 1],
            send_sem=s2.at[k - 1], recv_sem=r2.at[k - 1],
            device_id={EXCHANGE: lax.rem(me_b + k, n_b)}, device_id_type=MESH,
        )

    for k in range(1, n_b):
        p2(k).start()
    parts = [unpack(p2send, width)]
    for k in range(1, n_b):
        p2(k).wait_recv()
        parts.append(unpack(p2recv.at[k - 1], width))
    sums, _, totals = combine(parts)
    attended[me_a] = (sums / totals).astype(BF16)

    def p3(k):
        return pltpu.make_async_remote_copy(
            src_ref=attended.at[me_a], dst_ref=attended.at[me_a],
            send_sem=s3.at[k - 1], recv_sem=r3.at[k - 1],
            device_id={SCATTER: lax.rem(me_a + k, n_a)}, device_id_type=MESH,
        )

    for k in range(1, n_a):
        p3(k).start()
    for k in range(1, n_a):
        p3(k).wait_recv()
    projected = dot(attended[...].reshape(n_a * block, width), wo[...])
    dec[...] = layer_norm(qs[...].astype(F32) + projected[:n_query])

    for index in range(8):
        copy, there, comes, dst = halos[index]

        @pl.when(there)
        def _():
            copy.wait_send()

    for k in range(1, n_a):
        p1(k).wait_send()
        p3(k).wait_send()
    for k in range(1, n_b):
        p2(k).wait_send()


def body(sizes, features, dw_kernel, norm_gain, query_state, query_pos, wq, wk, wv, wo):
    tile_rows, tile_cols, width = features.shape
    n_query = query_state.shape[0]
    n_a, n_b = sizes[SCATTER], sizes[EXCHANGE]
    block = -(-n_query // (16 * n_a)) * 16
    pixels = tile_rows * tile_cols
    row_bytes = width + STATS
    vmem = pl.BlockSpec(memory_space=pltpu.VMEM)
    dma = pltpu.SemaphoreType.DMA
    return pl.pallas_call(
        functools.partial(kernel, sizes),
        out_shape=(
            jax.ShapeDtypeStruct(features.shape, BF16),
            jax.ShapeDtypeStruct((n_query, width), F32),
        ),
        in_specs=[vmem] * 9,
        out_specs=(vmem, vmem),
        scratch_shapes=[
            pltpu.VMEM((tile_rows + 6, tile_cols + 16, width), F32),
            pltpu.VMEM((7, 7, width), F32),
            pltpu.VMEM((8, tile_cols, width), F32),
            pltpu.VMEM((6 * tile_rows + 64, width), BF16),
            pltpu.VMEM((2, 3, tile_cols, width), BF16),
            pltpu.VMEM((2, 3 * tile_rows, width), BF16),
            pltpu.VMEM((4, 16, width), BF16),
            pltpu.VMEM((pixels, width), BF16),
            pltpu.VMEM((pixels, width), BF16),
            pltpu.VMEM((n_a * block, width), F32),
            pltpu.VMEM((n_a * block, width), BF16),
            pltpu.VMEM((n_a - 1, block, row_bytes), BF16),
            pltpu.VMEM((n_a - 1, block, row_bytes), BF16),
            pltpu.VMEM((block, row_bytes), BF16),
            pltpu.VMEM((n_b - 1, block, row_bytes), BF16),
            pltpu.VMEM((n_a, block, width), BF16),
            dma((8,)), dma((8,)),
            dma((n_a - 1,)), dma((n_a - 1,)),
            dma((n_b - 1,)), dma((n_b - 1,)),
            dma((n_a - 1,)), dma((n_a - 1,)),
        ],
        compiler_params=pltpu.CompilerParams(
            collective_id=0, has_side_effects=True, vmem_limit_bytes=40 * 1024 * 1024
        ),
    )(features, dw_kernel, norm_gain.reshape(1, width), query_state, query_pos, wq, wk, wv, wo)


def solution(mesh):
    sizes = dict(mesh.shape)
    in_specs = (
        P(("scenes", "rows"), "cols", None),
        P(),
        P(),
        P("scenes", None),
        P("scenes", None),
        P(),
        P(),
        P(),
        P(),
    )
    out_specs = (P(("scenes", "rows"), "cols", None), P("scenes", None))
    return jax.shard_map(
        functools.partial(body, sizes), mesh=mesh, in_specs=in_specs, out_specs=out_specs,
        check_vma=False,
    )
```

time: 220 us -> 41.7 us (0.19)
  blocking collectives: 118 us -> 0 us
  waiting for transfers between devices: 38.9 us -> 0 us
  Pallas kernels: 0 us -> 31.4 us
  matrix products: 14.5 us -> 0 us
  other arithmetic: 14.5 us -> 0 us
  between operations: 14.4 us -> 0.66 us
  starting transfers between devices: 8.45 us -> 0 us
    pmax x1 -> x0, blocking collectives: 59.7 us -> none  [body(): global_max = lax.pmax(maxima, ('rows', 'cols'))]
    psum x1 -> x0, blocking collectives: 58.2 us -> none  [body(): lax.psum((totals * rescale, sums * widen(rescale)), ('rows', 'cols'))]
    psum x1 -> x0, waiting for transfers between devices: 32.4 us -> none  [body(): lax.psum((totals * rescale, sums * widen(rescale)), ('rows', 'cols'))]
    pallas_call x0 -> x1, Pallas kernels: none -> 31.4 us  [body(): pl.pallas_call(functools.partial(kernel, sizes), out_shape=(jax.ShapeDtyp...]
    dot_general x20 -> x0, matrix products: 14.5 us -> none  [the longest x8 7.25 us: body(): jnp.dot(expo.astype(jnp.bfloat16), values[:, low:low + head_dim], preferr...]
    reduce_sum x11 -> x0, other arithmetic: 10.6 us -> none  [the longest x1 6.16 us: layer_norm(): centred = vector - jnp.mean(vector, axis=-1, keepdims=True)]
    ppermute x4 -> x0, starting transfers between devices: 8.41 us -> none  [the longest x2 5.83 us: with_halo(): before = lax.ppermute(last, axis, up)]
    unnamed x49 -> x20, local copies, waits for them, and re-layouts: 1.21 us -> 9.23 us
  transfers between devices with their start and end apart: 5 -> 0, of which waited for: 4 -> 0; matrix products, arithmetic and copies ran while one was open for 1% -> 0% of each run, Pallas kernels for 0% -> 0%
where the time goes in v1:
time: 41.7 us; the launch traced here: 41.3 us
  Pallas kernels  31.4 us (75%)
  local copies, waits for them, and re-layouts  9.23 us (22%)
  between operations  0.66 us (2%)
    pallas_call x1, Pallas kernels, body(): pl.pallas_call(functools.partial(kernel, sizes), out_shape=(jax.ShapeDtyp...  31.4 us
    unnamed x20, local copies, waits for them, and re-layouts  9.23 us

profile of v1, /device:TPU:0, one launch (start us, length us, event | category | flops | bytes accessed | tf_op | source)
XLA Modules:
  0.0 41.3 jit_solution(15550616745327820214)
XLA Ops:
  0.6 0.0 copy-start.8
  0.6 0.7 %copy-done.8 = f32[256]{0:T(256)S(1)} copy-done((f32[256]{0:T(256)S(1)}, f32[256]{0:T(256)}, u32[]{:S(2)}) %copy-start.8) | copy-done | bytes 1048
  1.3 0.0 copy-start
  1.3 0.9 %copy-done = bf16[32,16,256]{2,1,0:T(8,128)(2,1)S(1)} copy-done((bf16[32,16,256]{2,1,0:T(8,128)(2,1)S(1)}, bf16[32,16,256]{2,1,0:T(8,128)(2,1)}, u32[]{:S(2)}) %copy-start) | copy-done | bytes 262168
  2.3 0.0 copy-start.1
  2.3 0.9 %copy-done.1 = bf16[300,256]{1,0:T(8,128)(2,1)S(1)} copy-done((bf16[300,256]{1,0:T(8,128)(2,1)S(1)}, bf16[300,256]{1,0:T(8,128)(2,1)}, u32[]{:S(2)}) %copy-start.1) | copy-done | bytes 153624
  3.2 0.0 copy-start.2
  3.2 0.9 %copy-done.2 = bf16[300,256]{1,0:T(8,128)(2,1)S(1)} copy-done((bf16[300,256]{1,0:T(8,128)(2,1)S(1)}, bf16[300,256]{1,0:T(8,128)(2,1)}, u32[]{:S(2)}) %copy-start.2) | copy-done | bytes 153624
  4.1 0.0 copy-start.3
  4.1 0.9 %copy-done.3 = bf16[256,256]{1,0:T(8,128)(2,1)S(1)} copy-done((bf16[256,256]{1,0:T(8,128)(2,1)S(1)}, bf16[256,256]{1,0:T(8,128)(2,1)}, u32[]{:S(2)}) %copy-start.3) | copy-done | bytes 131096
  5.0 0.0 copy-start.4
  5.0 0.9 %copy-done.4 = bf16[256,256]{1,0:T(8,128)(2,1)S(1)} copy-done((bf16[256,256]{1,0:T(8,128)(2,1)S(1)}, bf16[256,256]{1,0:T(8,128)(2,1)}, u32[]{:S(2)}) %copy-start.4) | copy-done | bytes 131096
  5.9 0.0 copy-start.5
  5.9 0.9 %copy-done.5 = bf16[256,256]{1,0:T(8,128)(2,1)S(1)} copy-done((bf16[256,256]{1,0:T(8,128)(2,1)S(1)}, bf16[256,256]{1,0:T(8,128)(2,1)}, u32[]{:S(2)}) %copy-start.5) | copy-done | bytes 131096
  6.8 0.0 copy-start.6
  6.8 0.9 %copy-done.6 = bf16[256,256]{1,0:T(8,128)(2,1)S(1)} copy-done((bf16[256,256]{1,0:T(8,128)(2,1)S(1)}, bf16[256,256]{1,0:T(8,128)(2,1)}, u32[]{:S(2)}) %copy-start.6) | copy-done | bytes 131096
  7.7 0.0 copy-start.7
  7.7 0.7 %copy-done.7 = bf16[7,7,256]{2,1,0:T(8,128)(2,1)S(1)} copy-done((bf16[7,7,256]{2,1,0:T(8,128)(2,1)S(1)}, bf16[7,7,256]{2,1,0:T(8,128)(2,1)}, u32[]{:S(2)}) %copy-start.7) | copy-done | bytes 25112
  8.5 31.4 %shard_map.104 = (bf16[32,16,256]{2,1,0:T(8,128)(2,1)S(1)}, f32[300,256]{1,0:T(8,128)S(1)}) custom-call(bf16[32,16,256]{2,1,0:T(8,128)(2,1)S(1)} %copy-done, bf16[7,7,256]{2,1,0:T(8,128)(2,1)S(1)} %copy-done.7, f32[1,256]{1,0:T(1,128)S(1)} %bitcast.1, bf16[300,256]{1,0:T(8,128)(2,1)S(1)} %copy-done.1, bf16[300,256]{1,0:T(8,128)(2,1)S(1)} %copy-done.2, ...), custom_call_target="tpu_custom_call" | custom-call | tf_op jit(solution)/shard_map/pallas_call | solution.py:338
  39.9 0.7 %copy.13 = bf16[32,16,256]{2,1,0:T(8,128)(2,1)} copy(bf16[32,16,256]{2,1,0:T(8,128)(2,1)S(1)} %get-tuple-element.4) | data formatting | bytes 524288
  40.6 0.7 %copy.14 = f32[300,256]{1,0:T(8,128)} copy(f32[300,256]{1,0:T(8,128)S(1)} %get-tuple-element.5) | data formatting | bytes 614400
Async XLA Ops:
  0.6 0.7 %copy-start.8 = (f32[256]{0:T(256)S(1)}, f32[256]{0:T(256)}, u32[]{:S(2)}) copy-start(f32[256]{0:T(256)} %param.11) | copy-start | bytes 3076
  1.3 0.9 %copy-start = (bf16[32,16,256]{2,1,0:T(8,128)(2,1)S(1)}, bf16[32,16,256]{2,1,0:T(8,128)(2,1)}, u32[]{:S(2)}) copy-start(bf16[32,16,256]{2,1,0:T(8,128)(2,1)} %feat.1) | copy-start | bytes 786436
  2.3 0.9 %copy-start.1 = (bf16[300,256]{1,0:T(8,128)(2,1)S(1)}, bf16[300,256]{1,0:T(8,128)(2,1)}, u32[]{:S(2)}) copy-start(bf16[300,256]{1,0:T(8,128)(2,1)} %qs.1) | copy-start | bytes 460804
  3.2 0.9 %copy-start.2 = (bf16[300,256]{1,0:T(8,128)(2,1)S(1)}, bf16[300,256]{1,0:T(8,128)(2,1)}, u32[]{:S(2)}) copy-start(bf16[300,256]{1,0:T(8,128)(2,1)} %qp.1) | copy-start | bytes 460804
  4.1 0.9 %copy-start.3 = (bf16[256,256]{1,0:T(8,128)(2,1)S(1)}, bf16[256,256]{1,0:T(8,128)(2,1)}, u32[]{:S(2)}) copy-start(bf16[256,256]{1,0:T(8,128)(2,1)} %wq.1) | copy-start | bytes 393220
  5.0 0.9 %copy-start.4 = (bf16[256,256]{1,0:T(8,128)(2,1)S(1)}, bf16[256,256]{1,0:T(8,128)(2,1)}, u32[]{:S(2)}) copy-start(bf16[256,256]{1,0:T(8,128)(2,1)} %wk.1) | copy-start | bytes 393220
  5.9 0.9 %copy-start.5 = (bf16[256,256]{1,0:T(8,128)(2,1)S(1)}, bf16[256,256]{1,0:T(8,128)(2,1)}, u32[]{:S(2)}) copy-start(bf16[256,256]{1,0:T(8,128)(2,1)} %wv.1) | copy-start | bytes 393220
  6.8 0.9 %copy-start.6 = (bf16[256,256]{1,0:T(8,128)(2,1)S(1)}, bf16[256,256]{1,0:T(8,128)(2,1)}, u32[]{:S(2)}) copy-start(bf16[256,256]{1,0:T(8,128)(2,1)} %wo.1) | copy-start | bytes 393220
  7.7 0.7 %copy-start.7 = (bf16[7,7,256]{2,1,0:T(8,128)(2,1)S(1)}, bf16[7,7,256]{2,1,0:T(8,128)(2,1)}, u32[]{:S(2)}) copy-start(bf16[7,7,256]{2,1,0:T(8,128)(2,1)} %dwk.1) | copy-start | bytes 75268

commit v2 on v1

--- a/solution.py
+++ b/solution.py
@@ -85,8 +85,22 @@
 
 
 def kernel(
-    sizes, feat, dwk, gain, qs, qp, wq, wk, wv, wo, mem, dec,
-    pad, dwf, conv, packed, rowrecv, colrecv, cornrecv, keys, values, qf, queries,
+    sizes, *refs
+):
+    given, (mem, dec), rest = refs[:9], refs[9:11], refs[11:]
+    held, (insem, *rest) = rest[:9], rest[9:]
+    loads = {
+        name: pltpu.make_async_copy(given[i], held[i], insem.at[i])
+        for i, name in enumerate(("feat", "dwk", "gain", "qs", "qp", "wq", "wk", "wv", "wo"))
+    }
+    for name in ("feat", "qs", "qp", "wq", "dwk", "gain", "wk", "wv", "wo"):
+        loads[name].start()
+    main(sizes, loads, *held, mem, dec, *rest)
+
+
+def main(
+    sizes, loads, feat, dwk, gain, qs, qp, wq, wk, wv, wo, mem, dec,
+    pad, shifted, shift_sel, place_sel, dwf, conv, packed, rowrecv, colrecv, cornrecv, keys, values, qf, queries,
     p1send, p1recv, p2send, p2recv, attended,
     hsend, hrecv, s1, r1, s2, r2, s3, r3,
 ):
@@ -119,6 +133,7 @@
             device_id_type=MESH,
         )
 
+    loads["feat"].wait()
     flat_in = feat[...].reshape(pixels, width)
     pieces = []
     for first in (0, tile_cols - 3):
@@ -172,8 +187,42 @@
         def _():
             dst[...] = jnp.zeros(dst.shape, BF16)
 
-    pad[pl.ds(3, tile_rows), 8 : 8 + tile_cols, :] = feat[...].astype(F32)
+    wide = 2 * tile_cols
+
+    def place(step_q, step_k, shape, j_major):
+        q, k = iota(shape, 0), iota(shape, 1)
+        half = shape[1] // 2
+        is_right = k < half
+        k = jnp.where(k >= half, k - half, k)
+        if j_major:
+            j = jnp.where(k >= step_k, 1, 0) + jnp.where(k >= 2 * step_k, 1, 0)
+            r = k - j * step_k
+            fits = k >= 0
+        else:
+            j, r = k & 3, k >> 2
+            fits = (j < 3) & (r < 3)
+        hit = (q == r * step_q + j + jnp.where(is_right, 0, tile_cols - 3)) & fits
+        return jnp.where(hit, 1.0, 0.0).astype(BF16)
+
+    place_sel[...] = place(tile_cols, tile_rows, (pixels, 6 * tile_rows), True)
+    corner = place(tile_cols, 0, (3 * tile_cols, 32), False)
+    out, src = iota((8 * tile_cols, 8 * wide), 0), iota((8 * tile_cols, 8 * wide), 1)
+    out_row, out_col = out // tile_cols, out % tile_cols
+    shifts = []
+    for dc in range(7):
+        at = out_col + dc - 3
+        at = jnp.where(at < 0, at + wide, at)
+        shifts.append(jnp.where(src == out_row * wide + at, 1.0, 0.0).astype(BF16))
+    shift_sel[...] = jnp.concatenate(shifts, axis=0)
+    pad[tile_rows + 6 :] = jnp.zeros((pad.shape[0] - tile_rows - 6, wide, width), BF16)
+
+    pad[pl.ds(3, tile_rows), :tile_cols, :] = feat[...]
+    loads["dwk"].wait()
+    loads["gain"].wait()
     dwf[...] = dwk[...].astype(F32)
+    loads["qs"].wait()
+    loads["qp"].wait()
+    loads["wq"].wait()
     mixed = (qs[...].astype(F32) + qp[...].astype(F32)).astype(BF16)
     qf[...] = jnp.zeros(qf.shape, F32)
     qf[0:n_query, :] = dot(mixed, wq[...]) * head_dim ** (-0.5)
@@ -188,23 +237,20 @@
 
     for index in range(2):
         at = 0 if DIRS[index][0] > 0 else tile_rows + 3
-        pad[at : at + 3, 8 : 8 + tile_cols, :] = rowrecv[index].astype(F32)
-    for index in range(2, 4):
-        k, q = iota((tile_rows * 8, 3 * tile_rows), 1), iota((tile_rows * 8, 3 * tile_rows), 0)
-        j = jnp.where(k >= tile_rows, 1, 0) + jnp.where(k >= 2 * tile_rows, 1, 0)
-        left = DIRS[index][1] > 0
-        hit = q == (k - j * tile_rows) * 8 + j + (5 if left else 0)
-        slab = dot(jnp.where(hit, 1.0, 0.0).astype(BF16), colrecv[index - 2])
-        at = 0 if left else 8 + tile_cols
-        pad[3 : 3 + tile_rows, at : at + 8, :] = slab.reshape(tile_rows, 8, width)
-    for index in range(4, 8):
-        k, q = iota((24, 16), 1), iota((24, 16), 0)
-        left = DIRS[index][1] > 0
-        hit = (q == (k >> 2) * 8 + (k & 3) + (5 if left else 0)) & (k < 12) & ((k & 3) < 3)
-        slab = dot(jnp.where(hit, 1.0, 0.0).astype(BF16), cornrecv[index - 4])
-        up = 0 if DIRS[index][0] > 0 else tile_rows + 3
-        at = 0 if left else 8 + tile_cols
-        pad[up : up + 3, at : at + 8, :] = slab.reshape(3, 8, width)
+        pad[at : at + 3, :tile_cols, :] = rowrecv[index]
+
+    slab = dot(
+        place_sel[...],
+        colrecv[...].reshape(6 * tile_rows, width),
+    ).astype(BF16)
+    pad[pl.ds(3, tile_rows), tile_cols:, :] = slab.reshape(tile_rows, tile_cols, width)
+    for first, at in ((0, tile_rows + 3), (2, 0)):
+        slab = dot(corner, cornrecv[first : first + 2].reshape(32, width)).astype(BF16)
+        pad[at : at + 3, tile_cols:, :] = slab.reshape(3, tile_cols, width)
+
+    for group in range(pad.shape[0] // 8):
+        moved = dot(shift_sel[...], pad[8 * group : 8 * group + 8].reshape(8 * wide, width))
+        shifted[:, 8 * group : 8 * group + 8] = moved.reshape(7, 8, tile_cols, width)
 
     chunk = 8
     scale = gain[...]
@@ -218,7 +264,7 @@
                     jnp.broadcast_to(dwf[dr, dc : dc + 1, :], (8, width)) for dr in range(7)
                 ]
                 for i in range(chunk + 6):
-                    x = pad[r0 + i, 5 + dc + 8 * g : 13 + dc + 8 * g, :]
+                    x = shifted[dc, r0 + i, 8 * g : 8 * g + 8, :]
                     for dr in range(7):
                         o = i - dr
                         if 0 <= o < chunk:
@@ -233,6 +279,8 @@
 
     lax.fori_loop(0, tile_rows // chunk, conv_chunk, 0)
 
+    loads["wk"].wait()
+    loads["wv"].wait()
     flat = mem[...].reshape(pixels, width)
     keys[...] = dot(flat, wk[...]).astype(BF16)
     values[...] = dot(flat, wv[...]).astype(BF16)
@@ -309,6 +357,7 @@
         p3(k).start()
     for k in range(1, n_a):
         p3(k).wait_recv()
+    loads["wo"].wait()
     projected = dot(attended[...].reshape(n_a * block, width), wo[...])
     dec[...] = layer_norm(qs[...].astype(F32) + projected[:n_query])
 
@@ -335,16 +384,23 @@
     row_bytes = width + STATS
     vmem = pl.BlockSpec(memory_space=pltpu.VMEM)
     dma = pltpu.SemaphoreType.DMA
+    given = (
+        features, dw_kernel, norm_gain.reshape(1, width), query_state, query_pos, wq, wk, wv, wo
+    )
     return pl.pallas_call(
         functools.partial(kernel, sizes),
         out_shape=(
             jax.ShapeDtypeStruct(features.shape, BF16),
             jax.ShapeDtypeStruct((n_query, width), F32),
         ),
-        in_specs=[vmem] * 9,
+        in_specs=[pl.BlockSpec(memory_space=pltpu.HBM)] * 9,
         out_specs=(vmem, vmem),
-        scratch_shapes=[
-            pltpu.VMEM((tile_rows + 6, tile_cols + 16, width), F32),
+        scratch_shapes=[pltpu.VMEM(x.shape, x.dtype) for x in given] + [
+            dma((9,)),
+            pltpu.VMEM((tile_rows + 8, 2 * tile_cols, width), BF16),
+            pltpu.VMEM((7, tile_rows + 8, tile_cols, width), F32),
+            pltpu.VMEM((7 * 8 * tile_cols, 16 * tile_cols), BF16),
+            pltpu.VMEM((pixels, 6 * tile_rows), BF16),
             pltpu.VMEM((7, 7, width), F32),
             pltpu.VMEM((8, tile_cols, width), F32),
             pltpu.VMEM((6 * tile_rows + 64, width), BF16),
@@ -366,9 +422,9 @@
             dma((n_a - 1,)), dma((n_a - 1,)),
         ],
         compiler_params=pltpu.CompilerParams(
-            collective_id=0, has_side_effects=True, vmem_limit_bytes=40 * 1024 * 1024
+            collective_id=0, has_side_effects=True, vmem_limit_bytes=62 * 1024 * 1024
         ),
-    )(features, dw_kernel, norm_gain.reshape(1, width), query_state, query_pos, wq, wk, wv, wo)
+    )(*given)
 
 
 def solution(mesh):

time: 41.7 us -> 34.3 us (0.82)
  local copies, waits for them, and re-layouts: 9.23 us -> 2.44 us
    unnamed x20 -> x4, local copies, waits for them, and re-layouts: 9.23 us -> 2.44 us
where the time goes in v2:
time: 34.3 us; the launch traced here: 34.2 us
  Pallas kernels  31.1 us (91%)
  local copies, waits for them, and re-layouts  2.44 us (7%)
  between operations  0.65 us (2%)
    pallas_call x1, Pallas kernels, body(): pl.pallas_call(functools.partial(kernel, sizes), out_shape=(jax.ShapeDtyp...  31.1 us
    unnamed x4, local copies, waits for them, and re-layouts  2.44 us

profile of v2, /device:TPU:0, one launch (start us, length us, event | category | flops | bytes accessed | tf_op | source)
XLA Modules:
  0.0 34.2 jit_solution(9491677906777903932)
XLA Ops:
  0.6 31.1 %shard_map.104 = (bf16[32,16,256]{2,1,0:T(8,128)(2,1)}, f32[300,256]{1,0:T(8,128)}) custom-call(bf16[32,16,256]{2,1,0:T(8,128)(2,1)} %refs_0_.1, bf16[7,7,256]{2,1,0:T(8,128)(2,1)} %refs_1_.1, f32[1,256]{1,0:T(1,128)} %bitcast.1, bf16[300,256]{1,0:T(8,128)(2,1)} %refs_3_.1, bf16[300,256]{1,0:T(8,128)(2,1)} %refs_4_.1, bf16[256,256]{1,0:T(8,128)(2,1)} %refs_5_.1, ...), custom_call_target="tpu_custom_call" | custom-call | tf_op jit(solution)/shard_map/pallas_call | solution.py:390
  31.7 0.0 copy-start
  31.7 1.7 %copy.13 = bf16[32,16,256]{2,1,0:T(8,128)(2,1)} copy(bf16[32,16,256]{2,1,0:T(8,128)(2,1)} %get-tuple-element.4) | data formatting | bytes 524288
  33.5 0.0 copy-done
  33.5 0.7 %copy.14 = f32[300,256]{1,0:T(8,128)} copy(f32[300,256]{1,0:T(8,128)S(1)} %copy-done) | data formatting | bytes 614400
Async XLA Ops:
  31.7 1.7 %copy-start = (f32[300,256]{1,0:T(8,128)S(1)}, f32[300,256]{1,0:T(8,128)}, u32[]{:S(2)}) copy-start(f32[300,256]{1,0:T(8,128)} %get-tuple-element.5) | copy-start | bytes 921604

commit v3 on v2

--- a/solution.py
+++ b/solution.py
@@ -12,7 +12,8 @@
 MESH = pl.DeviceIdType.MESH
 F32 = jnp.float32
 BF16 = jnp.bfloat16
-STATS = 128
+TERMS = 6
+FOLD = 5
 
 DIRS = ((-1, 0), (1, 0), (0, -1), (0, 1), (-1, -1), (-1, 1), (1, -1), (1, 1))
 
@@ -40,35 +41,60 @@
     return parts
 
 
-def pack(out_ref, sums, maxima, totals):
-    width = sums.shape[1]
+def stat_rows(block):
+    return -(-block // (16 * FOLD)) * 16
+
+
+def make_picks(to_stats, to_wide):
+    width = to_stats.shape[1]
     head_dim = width // HEADS
-    out_ref[:, :width] = sums.astype(BF16)
-    src, lane = iota((width, STATS), 0), iota((width, STATS), 1)
+    src, lane = iota((width, width), 0), iota((width, width), 1)
+    for group in range(TERMS):
+        head = lane - group * HEADS
+        hit = (src == head * head_dim) & (head >= 0) & (head < HEADS)
+        to_stats[group] = jnp.where(hit, 1.0, 0.0).astype(BF16)
+    for which in range(2):
+        pick = None
+        for group in range(3 * which, 3 * which + 3):
+            head = src - group * HEADS
+            hit = (lane >= head * head_dim) & (lane < (head + 1) * head_dim)
+            hit = hit & (head >= 0) & (head < HEADS)
+            pick = hit if pick is None else pick | hit
+        to_wide[which] = jnp.where(pick, 1.0, 0.0).astype(BF16)
+
+
+def pack(to_stats, out_ref, sums, maxima, totals):
+    block, width = sums.shape
+    out_ref[:block] = sums.astype(BF16)
     stats = None
     for group, part in enumerate(split(maxima, 3) + split(totals, 3)):
-        pick = (src == (lane - group * HEADS) * head_dim) & (lane >= group * HEADS)
-        pick = pick & (lane < (group + 1) * HEADS)
-        term = dot(part, jnp.where(pick, 1.0, 0.0).astype(BF16))
+        term = dot(part, to_stats[group])
         stats = term if stats is None else stats + term
-    out_ref[:, width:] = stats.astype(BF16)
-
-
-def unpack(in_ref, width):
-    head_dim = width // HEADS
-    sums = in_ref[:, :width].astype(F32)
-    stats = in_ref[:, width:]
-    lane, chan = iota((STATS, width), 0), iota((STATS, width), 1)
-    results = [sums]
-    for first in (0, 3 * HEADS):
-        pick = None
-        for group in range(3):
-            head = lane - (first + group * HEADS)
-            hit = (chan >= head * head_dim) & (chan < (head + 1) * head_dim)
-            hit = hit & (head >= 0) & (head < HEADS)
-            pick = hit if pick is None else pick | hit
-        results.append(dot(stats, jnp.where(pick, 1.0, 0.0).astype(BF16)))
-    return results
+    span = TERMS * HEADS
+    for first in range(0, block // 16, FOLD):
+        folded = None
+        for t in range(first, min(first + FOLD, block // 16)):
+            part = stats[16 * t : 16 * t + 16]
+            if t > first:
+                part = pltpu.roll(part, span * (t - first), 1)
+            folded = part if folded is None else folded + part
+        at = block + 16 * (first // FOLD)
+        out_ref[at : at + 16] = folded.astype(BF16)
+
+
+def unpack(to_wide, in_ref, block):
+    width = in_ref.shape[1]
+    sums = in_ref[:block].astype(F32)
+    span = TERMS * HEADS
+    rows = []
+    for t in range(block // 16):
+        at = block + 16 * (t // FOLD)
+        part = in_ref[at : at + 16].astype(F32)
+        if t % FOLD:
+            part = pltpu.roll(part, width - span * (t % FOLD), 1)
+        rows.append(part)
+    stats = jnp.concatenate(rows, axis=0).astype(BF16)
+    return sums, dot(stats, to_wide[0]), dot(stats, to_wide[1])
 
 
 def combine(parts):
@@ -100,7 +126,7 @@
 
 def main(
     sizes, loads, feat, dwk, gain, qs, qp, wq, wk, wv, wo, mem, dec,
-    pad, shifted, shift_sel, place_sel, dwf, conv, packed, rowrecv, colrecv, cornrecv, keys, values, qf, queries,
+    to_stats, to_wide, pad, shifted, shift_sel, place_sel, dwf, conv, packed, rowrecv, colrecv, cornrecv, keys, values, qf, queries,
     p1send, p1recv, p2send, p2recv, attended,
     hsend, hrecv, s1, r1, s2, r2, s3, r3,
 ):
@@ -109,7 +135,7 @@
     tile_rows, tile_cols, width = feat.shape
     pixels = tile_rows * tile_cols
     n_query = qs.shape[0]
-    block = p2send.shape[0]
+    block = attended.shape[1]
     head_dim = width // HEADS
     row, col = lax.axis_index("rows"), lax.axis_index("cols")
     me_a, me_b = lax.axis_index(SCATTER), lax.axis_index(EXCHANGE)
@@ -187,6 +213,7 @@
         def _():
             dst[...] = jnp.zeros(dst.shape, BF16)
 
+    make_picks(to_stats, to_wide)
     wide = 2 * tile_cols
 
     def place(step_q, step_k, shape, j_major):
@@ -318,7 +345,7 @@
 
     def scatter_step(step, carry):
         k = step + 1
-        pack(p1send.at[step], *attend(lax.rem(me_a + k, n_a)))
+        pack(to_stats, p1send.at[step], *attend(lax.rem(me_a + k, n_a)))
         p1(k).start()
         return carry
 
@@ -326,9 +353,9 @@
     parts = [attend(me_a)]
     for k in range(1, n_a):
         p1(k).wait_recv()
-        parts.append(unpack(p1recv.at[k - 1], width))
+        parts.append(unpack(to_wide, p1recv.at[k - 1], block))
     mine = combine(parts)
-    pack(p2send, *mine)
+    pack(to_stats, p2send, *mine)
 
     def p2(k):
         return pltpu.make_async_remote_copy(
@@ -339,10 +366,10 @@
 
     for k in range(1, n_b):
         p2(k).start()
-    parts = [unpack(p2send, width)]
+    parts = [unpack(to_wide, p2send, block)]
     for k in range(1, n_b):
         p2(k).wait_recv()
-        parts.append(unpack(p2recv.at[k - 1], width))
+        parts.append(unpack(to_wide, p2recv.at[k - 1], block))
     sums, _, totals = combine(parts)
     attended[me_a] = (sums / totals).astype(BF16)
 
@@ -381,7 +408,7 @@
     n_a, n_b = sizes[SCATTER], sizes[EXCHANGE]
     block = -(-n_query // (16 * n_a)) * 16
     pixels = tile_rows * tile_cols
-    row_bytes = width + STATS
+    message = block + stat_rows(block)
     vmem = pl.BlockSpec(memory_space=pltpu.VMEM)
     dma = pltpu.SemaphoreType.DMA
     given = (
@@ -397,6 +424,8 @@
         out_specs=(vmem, vmem),
         scratch_shapes=[pltpu.VMEM(x.shape, x.dtype) for x in given] + [
             dma((9,)),
+            pltpu.VMEM((TERMS, width, width), BF16),
+            pltpu.VMEM((2, width, width), BF16),
             pltpu.VMEM((tile_rows + 8, 2 * tile_cols, width), BF16),
             pltpu.VMEM((7, tile_rows + 8, tile_cols, width), F32),
             pltpu.VMEM((7 * 8 * tile_cols, 16 * tile_cols), BF16),
@@ -411,10 +440,10 @@
             pltpu.VMEM((pixels, width), BF16),
             pltpu.VMEM((n_a * block, width), F32),
             pltpu.VMEM((n_a * block, width), BF16),
-            pltpu.VMEM((n_a - 1, block, row_bytes), BF16),
-            pltpu.VMEM((n_a - 1, block, row_bytes), BF16),
-            pltpu.VMEM((block, row_bytes), BF16),
-            pltpu.VMEM((n_b - 1, block, row_bytes), BF16),
+            pltpu.VMEM((n_a - 1, message, width), BF16),
+            pltpu.VMEM((n_a - 1, message, width), BF16),
+            pltpu.VMEM((message, width), BF16),
+            pltpu.VMEM((n_b - 1, message, width), BF16),
             pltpu.VMEM((n_a, block, width), BF16),
             dma((8,)), dma((8,)),
             dma((n_a - 1,)), dma((n_a - 1,)),

time: 34.3 us -> 33.6 us (0.980)
  Pallas kernels: 31.1 us -> 30.4 us
    pallas_call x1, Pallas kernels: 31.1 us -> 30.4 us  [body(): pl.pallas_call(functools.partial(kernel, sizes), out_shape=(jax.ShapeDtyp...]
where the time goes in v3:
time: 33.6 us; the launch traced here: 33.5 us
  Pallas kernels  30.4 us (90%)
  local copies, waits for them, and re-layouts  2.44 us (7%)
  between operations  0.65 us (2%)
    pallas_call x1, Pallas kernels, body(): pl.pallas_call(functools.partial(kernel, sizes), out_shape=(jax.ShapeDtyp...  30.4 us
    unnamed x4, local copies, waits for them, and re-layouts  2.44 us

profile of v3, /device:TPU:0, one launch (start us, length us, event | category | flops | bytes accessed | tf_op | source)
XLA Modules:
  0.0 33.5 jit_solution(8771141078113802830)
XLA Ops:
  0.6 30.4 %shard_map.104 = (bf16[32,16,256]{2,1,0:T(8,128)(2,1)}, f32[300,256]{1,0:T(8,128)}) custom-call(bf16[32,16,256]{2,1,0:T(8,128)(2,1)} %refs_0_.1, bf16[7,7,256]{2,1,0:T(8,128)(2,1)} %refs_1_.1, f32[1,256]{1,0:T(1,128)} %bitcast.1, bf16[300,256]{1,0:T(8,128)(2,1)} %refs_3_.1, bf16[300,256]{1,0:T(8,128)(2,1)} %refs_4_.1, bf16[256,256]{1,0:T(8,128)(2,1)} %refs_5_.1, ...), custom_call_target="tpu_custom_call" | custom-call | tf_op jit(solution)/shard_map/pallas_call | solution.py:417
  31.0 0.0 copy-start
  31.0 1.7 %copy.13 = bf16[32,16,256]{2,1,0:T(8,128)(2,1)} copy(bf16[32,16,256]{2,1,0:T(8,128)(2,1)} %get-tuple-element.4) | data formatting | bytes 524288
  32.7 0.0 copy-done
  32.7 0.7 %copy.14 = f32[300,256]{1,0:T(8,128)} copy(f32[300,256]{1,0:T(8,128)S(1)} %copy-done) | data formatting | bytes 614400
Async XLA Ops:
  31.0 1.7 %copy-start = (f32[300,256]{1,0:T(8,128)S(1)}, f32[300,256]{1,0:T(8,128)}, u32[]{:S(2)}) copy-start(f32[300,256]{1,0:T(8,128)} %get-tuple-element.5) | copy-start | bytes 921604

commit v4 on v3

--- a/solution.py
+++ b/solution.py
@@ -279,32 +279,36 @@
         moved = dot(shift_sel[...], pad[8 * group : 8 * group + 8].reshape(8 * wide, width))
         shifted[:, 8 * group : 8 * group + 8] = moved.reshape(7, 8, tile_cols, width)
 
-    chunk = 8
     scale = gain[...]
-
-    def conv_chunk(step, carry):
-        r0 = step * chunk
-        for g in range(tile_cols // 8):
-            acc = [jnp.zeros((8, width), F32) for _ in range(chunk)]
-            for dc in range(7):
-                taps = [
-                    jnp.broadcast_to(dwf[dr, dc : dc + 1, :], (8, width)) for dr in range(7)
-                ]
-                for i in range(chunk + 6):
-                    x = shifted[dc, r0 + i, 8 * g : 8 * g + 8, :]
-                    for dr in range(7):
-                        o = i - dr
-                        if 0 <= o < chunk:
-                            acc[o] = acc[o] + x * taps[dr]
-            for o in range(chunk):
-                conv[o, 8 * g : 8 * g + 8, :] = acc[o]
-        normed = layer_norm(conv[...].reshape(chunk * tile_cols, width))
-        image = feat[pl.ds(r0, chunk)].astype(F32).reshape(chunk * tile_cols, width)
-        result = (image + normed * scale).astype(BF16)
-        mem[pl.ds(r0, chunk)] = result.reshape(chunk, tile_cols, width)
-        return carry
-
-    lax.fori_loop(0, tile_rows // chunk, conv_chunk, 0)
+    half = width // 2
+
+    for g in range(tile_cols // 8):
+        for lanes in (slice(0, half), slice(half, width)):
+
+            def rows_step(step, carry):
+                r0 = step * 16
+                acc = [jnp.zeros((8, half), F32) for _ in range(16)]
+                for dc in range(7):
+                    taps = [
+                        jnp.broadcast_to(dwf[dr, dc : dc + 1, lanes], (8, half))
+                        for dr in range(7)
+                    ]
+                    for i in range(22):
+                        x = shifted[dc, r0 + i, 8 * g : 8 * g + 8, lanes]
+                        for dr in range(7):
+                            o = i - dr
+                            if 0 <= o < 16:
+                                acc[o] = acc[o] + x * taps[dr]
+                for o in range(16):
+                    conv[r0 + o, 8 * g : 8 * g + 8, lanes] = acc[o]
+                return carry
+
+            lax.fori_loop(0, tile_rows // 16, rows_step, 0, unroll=True)
+
+    normed = layer_norm(conv[...].reshape(pixels, width))
+    image = feat[...].astype(F32).reshape(pixels, width)
+    result = (image + normed * scale).astype(BF16)
+    mem[...] = result.reshape(tile_rows, tile_cols, width)
 
     loads["wk"].wait()
     loads["wv"].wait()
@@ -431,7 +435,7 @@
             pltpu.VMEM((7 * 8 * tile_cols, 16 * tile_cols), BF16),
             pltpu.VMEM((pixels, 6 * tile_rows), BF16),
             pltpu.VMEM((7, 7, width), F32),
-            pltpu.VMEM((8, tile_cols, width), F32),
+            pltpu.VMEM((tile_rows, tile_cols, width), F32),
             pltpu.VMEM((6 * tile_rows + 64, width), BF16),
             pltpu.VMEM((2, 3, tile_cols, width), BF16),
             pltpu.VMEM((2, 3 * tile_rows, width), BF16),

time: 33.6 us -> 31.6 us (0.940)
  Pallas kernels: 30.4 us -> 28.4 us
    pallas_call x1, Pallas kernels: 30.4 us -> 28.4 us  [body(): pl.pallas_call(functools.partial(kernel, sizes), out_shape=(jax.ShapeDtyp...]
where the time goes in v4:
time: 31.6 us; the launch traced here: 31.5 us
  Pallas kernels  28.4 us (90%)
  local copies, waits for them, and re-layouts  2.44 us (8%)
  between operations  0.65 us (2%)
    pallas_call x1, Pallas kernels, body(): pl.pallas_call(functools.partial(kernel, sizes), out_shape=(jax.ShapeDtyp...  28.4 us
    unnamed x4, local copies, waits for them, and re-layouts  2.44 us

profile of v4, /device:TPU:0, one launch (start us, length us, event | category | flops | bytes accessed | tf_op | source)
XLA Modules:
  0.0 31.5 jit_solution(8809435256024794776)
XLA Ops:
  0.6 28.4 %shard_map.104 = (bf16[32,16,256]{2,1,0:T(8,128)(2,1)}, f32[300,256]{1,0:T(8,128)}) custom-call(bf16[32,16,256]{2,1,0:T(8,128)(2,1)} %refs_0_.1, bf16[7,7,256]{2,1,0:T(8,128)(2,1)} %refs_1_.1, f32[1,256]{1,0:T(1,128)} %bitcast.1, bf16[300,256]{1,0:T(8,128)(2,1)} %refs_3_.1, bf16[300,256]{1,0:T(8,128)(2,1)} %refs_4_.1, bf16[256,256]{1,0:T(8,128)(2,1)} %refs_5_.1, ...), custom_call_target="tpu_custom_call" | custom-call | tf_op jit(solution)/shard_map/pallas_call | solution.py:421
  29.0 0.0 copy-start
  29.0 1.7 %copy.13 = bf16[32,16,256]{2,1,0:T(8,128)(2,1)} copy(bf16[32,16,256]{2,1,0:T(8,128)(2,1)} %get-tuple-element.4) | data formatting | bytes 524288
  30.8 0.0 copy-done
  30.8 0.7 %copy.14 = f32[300,256]{1,0:T(8,128)} copy(f32[300,256]{1,0:T(8,128)S(1)} %copy-done) | data formatting | bytes 614400
Async XLA Ops:
  29.0 1.7 %copy-start = (f32[300,256]{1,0:T(8,128)S(1)}, f32[300,256]{1,0:T(8,128)}, u32[]{:S(2)}) copy-start(f32[300,256]{1,0:T(8,128)} %get-tuple-element.5) | copy-start | bytes 921604
